TPU v7x, 256 devices: a whole 4x4x8 slice. The times are simulated.
256 devices in a mesh: ctx: 64 (over x, y, z_lo), tp: 4 (over z_hi, core).
Axes of the slice: x: 4, y: 4, z: 8 (z_hi: 2, z_lo: 4; z = z_hi * 4 + z_lo), core: 2. Of those that a mesh axis runs over, the one named last changes fastest.
Arguments:
- hidden: bfloat16 [32768, 8192], P('ctx'), may hold values from -32 to 32, as said below
- w_query: bfloat16 [8192, 4096], P('ctx', 'tp'), may hold values from -0.0625 to 0.0625
- w_key: bfloat16 [8192, 512], P('ctx', 'tp'), may hold values from -0.0625 to 0.0625
- w_value: bfloat16 [8192, 512], P('ctx', 'tp'), may hold values from -0.0625 to 0.0625
- block_order: int32 [64], replicated, may hold values from 0 to 63, each once
- page_map: int32 [4096, 1], replicated, may hold values from 0 to 63; in each aligned block of 64 rows (0 to 63, 64 to 127, ...) at most 2 rows name the same one
Outputs:
- attended: bfloat16 [32768, 4096], P('ctx', 'tp')
- kv_cache: bfloat16 [64, 64, 2, 8, 1024], P('ctx', None, None, None, 'tp')
Inputs may be any that keep to these rules, and one draw needn't show every extreme that they name: `hidden`: drawn activations; no further structure. `page_map`: among the 64 pages of one block, at most 2 share an owner, and in every draw some block has 2 pages with one owner. `block_order`: each block number appears once.
All inputs are finite; a program needn't handle non-finite values.
Results may differ from a plain program's by a relative error of at most 0.012.
The roundings to bfloat16 on the way count: a program that leaves them out, or rounds other values in their place, can miss the bound.
Values may be sent and summed in bfloat16 or wider, within the bound.
A program may use at most 128 MiB of HBM per device.

v0:
```python
import jax
import jax.numpy as jnp
from jax import lax
from jax.sharding import PartitionSpec as P

HD = 128
PAGE = 8


rope_theta = 500000.0
neg_large = -1e30


def spread(x, axis, root):
    mine = lax.axis_index(axis) == root
    return lax.psum(jnp.where(mine, x, jnp.zeros_like(x)), axis)


def rotate(values, positions):
    half_width = values.shape[-1] // 2
    exponent = jnp.arange(half_width, dtype=jnp.float32) * (2.0 / values.shape[-1])
    inverse = jnp.exp(-exponent * jnp.log(jnp.float32(rope_theta)))
    angles = positions[:, None] * inverse[None, :]
    cosine = jnp.cos(angles)
    sine = jnp.sin(angles)
    cosine = jnp.concatenate([cosine, cosine], -1)[:, None, :]
    sine = jnp.concatenate([sine, sine], -1)[:, None, :]
    lower_half = values[..., :half_width]
    upper_half = values[..., half_width:]
    turned = jnp.concatenate([-upper_half, lower_half], -1)
    return values * cosine + turned * sine


def attend_block(query_block, key_block, value_block, anchor_key, anchor_value, is_anchor):
    row_count = query_block.shape[0]
    score_scale = 1.0 / jnp.sqrt(jnp.float32(query_block.shape[-1]))
    own = (
        jnp.einsum("rkgd,skd->kgrs", query_block, key_block, preferred_element_type=jnp.float32)
        * score_scale
    )
    causal = jnp.arange(row_count)[:, None] >= jnp.arange(row_count)[None, :]
    own = jnp.where(causal, own, neg_large)
    far = (
        jnp.einsum("rkgd,skd->kgrs", query_block, anchor_key, preferred_element_type=jnp.float32)
        * score_scale
    )
    far = jnp.where(is_anchor, neg_large, far)
    top = jnp.maximum(jnp.max(own, -1), jnp.max(far, -1))
    own_exp = jnp.exp(own - top[..., None])
    far_exp = jnp.exp(far - top[..., None])
    total = jnp.sum(own_exp, -1) + jnp.sum(far_exp, -1)
    own_weights = (own_exp / total[..., None]).astype(jnp.bfloat16)
    far_weights = (far_exp / total[..., None]).astype(jnp.bfloat16)
    result = jnp.einsum(
        "kgrs,skd->rkgd", own_weights, value_block, preferred_element_type=jnp.float32
    )
    result = result + jnp.einsum(
        "kgrs,skd->rkgd", far_weights, anchor_value, preferred_element_type=jnp.float32
    )
    return result.reshape(row_count, -1).astype(jnp.bfloat16)


def on_device(hidden, w_query, w_key, w_value, block_order, page_map):
    row_count = hidden.shape[0]
    ctx_count = lax.axis_size("ctx")
    my_index = lax.axis_index("ctx")
    head_count = w_query.shape[1] // HD
    pair_heads = w_key.shape[1] // HD
    group_size = head_count // pair_heads

    def add_rows(piece):
        return jnp.dot(hidden, piece, preferred_element_type=jnp.float32)

    queries = add_rows(lax.all_gather(w_query, "ctx", axis=0, tiled=True))
    keys_raw = add_rows(lax.all_gather(w_key, "ctx", axis=0, tiled=True))
    values_raw = add_rows(lax.all_gather(w_value, "ctx", axis=0, tiled=True))
    my_block = block_order[my_index]
    positions = (my_block * row_count + jnp.arange(row_count, dtype=jnp.int32)).astype(jnp.float32)
    query_heads = rotate(queries.reshape(row_count, head_count, HD), positions).astype(jnp.bfloat16)
    query_heads = query_heads.reshape(row_count, pair_heads, group_size, HD)
    key_heads = rotate(keys_raw.reshape(row_count, pair_heads, HD), positions).astype(jnp.bfloat16)
    value_heads = values_raw.reshape(row_count, pair_heads, HD).astype(jnp.bfloat16)
    width = pair_heads * 2 * HD
    pair_pack = jnp.concatenate([key_heads, value_heads], -1).reshape(row_count, width)
    root_index = jnp.sum(jnp.where(block_order == 0, jnp.arange(ctx_count, dtype=jnp.int32), 0))
    anchor_pack = spread(pair_pack, "ctx", root_index)
    anchor_pack = anchor_pack.reshape(row_count, pair_heads, 2 * HD)
    anchor_key = anchor_pack[..., :HD]
    anchor_value = anchor_pack[..., HD:]
    attended = attend_block(
        query_heads, key_heads, value_heads, anchor_key, anchor_value, my_block == 0
    )
    page_count = row_count // PAGE
    capacity = max(2, 2 * page_count // ctx_count)
    owners = lax.dynamic_slice_in_dim(page_map[:, 0], my_block * page_count, page_count, 0)
    before = jnp.arange(page_count)[None, :] < jnp.arange(page_count)[:, None]
    earlier = (owners[:, None] == owners[None, :]) & before
    slot_rank = jnp.sum(jnp.where(earlier, 1, 0), axis=-1).astype(jnp.int32)
    owner_match = owners[None, None, :] == jnp.arange(ctx_count, dtype=jnp.int32)[:, None, None]
    slot_match = slot_rank[None, None, :] == jnp.arange(capacity, dtype=jnp.int32)[None, :, None]
    selector = (owner_match & slot_match).astype(jnp.bfloat16)
    page_rows = pair_pack.reshape(page_count, PAGE * width)
    outgoing = jnp.einsum(
        "osj,jx->osx", selector, page_rows, preferred_element_type=jnp.float32
    ).astype(jnp.bfloat16)
    incoming = lax.all_to_all(outgoing, "ctx", split_axis=0, concat_axis=0, tiled=True)
    reorder = (block_order[None, :] == jnp.arange(ctx_count, dtype=jnp.int32)[:, None]).astype(
        jnp.bfloat16
    )
    placed = jnp.einsum(
        "bc,csx->bsx", reorder, incoming, preferred_element_type=jnp.float32
    ).astype(jnp.bfloat16)
    kv_cache = placed.reshape(1, ctx_count, capacity, PAGE, width)
    return (attended, kv_cache)


def solution(mesh):
    placed = (P("ctx", None), P("ctx", "tp"), P("ctx", "tp"), P("ctx", "tp"), P(), P())
    return jax.shard_map(
        on_device,
        mesh=mesh,
        in_specs=placed,
        out_specs=(P("ctx", "tp"), P("ctx", None, None, None, "tp")),
        check_vma=False,
    )
```

profile of v0, /device:TPU:32, one launch (start us, length us, event | category | flops | bytes accessed | tf_op | source)
XLA Modules:
  0.0 1803.1 jit_solution(17064826122999081155)
XLA Ops:
  7.2 0.7 all-gather.6.cloned.1.call-update
  8.0 0.7 all-gather.4.cloned.1.call-update
  9.4 1.3 dynamic_slice.6
  10.7 1.3 fusion.34
  14.7 347.1 %all-gather.6.cloned.1.call-done = bf16[8192,128]{1,0:T(8,128)(2,1)} async-done(((bf16[128,128]{1,0:T(8,128)(2,1)}), bf16[8192,128]{1,0:T(8,128)(2,1)}) %all-gather.6.cloned.1.call-update) | async-done | bytes 2097168 | tf_op jit(solution)/shard_map/all_gather | solution.py:75
  361.8 6.9 fusion.39
  368.8 342.6 %all-gather.4.cloned.1.call-done = bf16[8192,128]{1,0:T(8,128)(2,1)} async-done(((bf16[128,128]{1,0:T(8,128)(2,1)}), bf16[8192,128]{1,0:T(8,128)(2,1)}) %all-gather.4.cloned.1.call-update) | async-done | bytes 2097168 | tf_op jit(solution)/shard_map/all_gather | solution.py:76
  711.4 6.9 convolution_convert_fusion.2
  718.2 0.8 pad_maximum_fusion.2
  719.6 1.3 copy.38
  720.9 9.9 all-to-all-start
  731.8 24.4 %all-to-all-done = bf16[64,2,2048]{2,1,0:T(2,128)(2,1)S(1)} async-done(((bf16[64,2,2048]{2,1,0:T(2,128)(2,1)}), bf16[64,2,2048]{2,1,0:T(2,128)(2,1)S(1)}, u32[]{:S(2)}, u32[]{:S(2)}) %all-to-all-start) | async-done | bytes 524320 | tf_op jit(solution)/shard_map/all_to_all | solution.py:106
  756.8 0.8 copy.41
  757.7 369.4 %all-gather.8.cloned.1.call-done = bf16[8192,1024]{1,0:T(8,128)(2,1)} async-done(((bf16[128,1024]{1,0:T(8,128)(2,1)}), bf16[8192,1024]{1,0:T(8,128)(2,1)}) %all-gather.8.cloned.1.call-update) | async-done | bytes 16777232 | tf_op jit(solution)/shard_map/all_gather | solution.py:74
  1127.1 14.3 fusion.40
  1143.3 1.3 fusion.14
  1144.6 4.9 fusion.3
  1149.5 633.3 %all-reduce.2.cloned.1.call-done = bf16[512,1,256]{0,2,1:T(8,128)(2,1)} async-done(((bf16[512,1,256]{0,2,1:T(8,128)(2,1)}), bf16[512,1,256]{0,2,1:T(8,128)(2,1)}) %all-reduce.2.cloned.1.call-update) | async-done | bytes 262160 | tf_op jit(solution)/shard_map/psum | solution.py:16
  1782.8 2.5 bitcast_reduce_fusion
  1785.3 0.9 copy-done.2
  1786.3 3.4 fusion.2
  1789.7 2.9 fusion.6
  1792.7 2.6 add_convert_fusion
  1795.3 1.3 copy.40
  (38 shorter events, 5.2 us)
Async XLA Ops:
  7.2 6.7 copy-start
  7.2 354.6 %all-gather.6.cloned.1.call-start = ((), (), s32[]{:S(2)}) async-start(), calls=%async_computation.2 | async-start | bytes 2129920 | tf_op jit(solution)/shard_map/all_gather | solution.py:75
  7.9 703.5 %all-gather.4.cloned.1.call-start = ((), (), s32[]{:S(2)}) async-start(), calls=%async_computation.1 | async-start | bytes 2129920 | tf_op jit(solution)/shard_map/all_gather | solution.py:76
  8.7 1118.5 %all-gather.8.cloned.1.call-start = ((), (), s32[]{:S(2)}) async-start(), calls=%async_computation.3 | async-start | bytes 17039360 | tf_op jit(solution)/shard_map/all_gather | solution.py:74
  368.8 387.5 %copy-start.4 = (s32[64]{0:T(128)S(1)}, s32[64]{0:T(128)}, u32[]{:S(2)}) copy-start(s32[64]{0:T(128)} %param.10) | copy-start | bytes 772
  720.9 35.3 %all-to-all-start = ((bf16[64,2,2048]{2,1,0:T(2,128)(2,1)}), bf16[64,2,2048]{2,1,0:T(2,128)(2,1)S(1)}, u32[]{:S(2)}, u32[]{:S(2)}) async-start(bf16[64,2,2048]{2,1,0:T(2,128)(2,1)} %copy.38), calls=%async_computation | async-start | bytes 1048576 | tf_op jit(solution)/shard_map/all_to_all | solution.py:106
  730.8 1052.1 %all-reduce.2.cloned.1.call-start = ((), (), s32[]{:S(2)}) async-start(), calls=%async_computation.4 | async-start | bytes 524288 | tf_op jit(solution)/shard_map/psum | solution.py:16
  1782.8 3.4 copy-start.2
  1789.7 3.0 copy-start.3
  1792.7 3.9 copy-start.1
Sparse Core Ops, SparseCore 0:
  9.8 351.9 all-gather.5
  363.6 347.7 all-gather.3
  713.2 413.9 all-gather.7
  1130.2 652.6 all-reduce.1
where the time goes:
time: 1800 us
  waiting for transfers between devices  1720 us (96%)
  matrix products  41.7 us (2%)
    psum x1, waiting for transfers between devices, spread(): return lax.psum(jnp.where(mine, x, jnp.zeros_like(x)), axis)  633 us
    all_gather x1, waiting for transfers between devices, on_device(): queries = add_rows(lax.all_gather(w_query, 'ctx', axis=0, tiled=True))  369 us
    all_gather x1, waiting for transfers between devices, on_device(): keys_raw = add_rows(lax.all_gather(w_key, 'ctx', axis=0, tiled=True))  347 us
    all_gather x1, waiting for transfers between devices, on_device(): values_raw = add_rows(lax.all_gather(w_value, 'ctx', axis=0, tiled=True))  343 us
  transfers between devices with their start and end apart: 5, of which 5 were waited for; matrix products, arithmetic and copies ran while one was open for 2% of the time, Pallas kernels for 0%

commit v1 on v0

v1 whole, which is shorter than its diff:
```python
import functools
import math

import jax
import jax.numpy as jnp
from jax import lax
from jax.experimental import pallas as pl
from jax.experimental.pallas import tpu as pltpu
from jax.sharding import PartitionSpec as P

HD = 128
PAGE = 8
TOK = 512
MESH = pl.DeviceIdType.MESH

rope_theta = 500000.0
neg_large = -1e30


def kernel(
    hidden, w_query, w_key, w_value, cosine, sine, page_src, source_of, flag,
    attended, kv_cache,
    W, hid, acc, ks, vs, qs, att, pg, p1, p2, p3, p4, m0, r0, m1, r1, m2, r2, r3, r4, kvo,
    loc, send, rec_a, rec_b, rec_c, line_s, line_r, page_s, page_r, page_l, anc_s, anc_r, out_s,
):
    c = lax.axis_index("ctx")
    x = c // 16
    y = (c // 4) % 4
    z = c % 4
    coords = {"x": x, "y": y, "z": z}

    def peer(axis, i):
        if axis == "x":
            return {"ctx": i * 16 + y * 4 + z}
        if axis == "y":
            return {"ctx": x * 16 + i * 4 + z}
        return {"ctx": x * 16 + y * 4 + i}

    def remote(src, dst, s, r, axis, i):
        pltpu.make_async_remote_copy(
            src_ref=src, dst_ref=dst, send_sem=s, recv_sem=r,
            device_id=peer(axis, i), device_id_type=MESH,
        ).start()

    def wait(ref, sem):
        pltpu.make_async_copy(ref, ref, sem).wait()

    def own_copy(g):
        if g == 0:
            src = w_key
        elif g == 1:
            src = w_value
        else:
            src = w_query.at[:, pl.ds((g - 2) * HD, HD)]
        return pltpu.make_async_copy(src, W.at[g, x, y, z], loc.at[g])

    hid_copies = [
        pltpu.make_async_copy(hidden.at[:, pl.ds(i * 2048, 2048)], hid.at[i], loc.at[10 + i])
        for i in range(4)
    ]
    for g in (0, 1, 8, 9, 2, 3, 4, 5, 6, 7):
        own_copy(g).start()

    barrier = pltpu.get_barrier_semaphore()
    for axis in "xyz":
        for d in (1, 2, 3):
            pl.semaphore_signal(
                barrier, inc=1, device_id=peer(axis, (coords[axis] + d) % 4), device_id_type=MESH
            )
    pl.semaphore_wait(barrier, 9)

    def first_axis(g):
        return "x" if g >= 8 else "z"

    def a_start(g):
        own_copy(g).wait()
        axis = first_axis(g)
        mine = W.at[g, x, y, z]
        for d in (1, 3, 2):
            remote(mine, mine, send.at[g, 0], rec_a.at[g], axis, (coords[axis] + d) % 4)

    def a_wait(g):
        wait(W.at[g, x, y, 0:3], rec_a.at[g])

    def layout(g, phase):
        if g >= 8:
            return "y", lambda i, h: W.at[g, pl.ds(2 * h, 2), i, z], lambda n: W.at[g, :, 0:n, z]
        if g % 2 == 0:
            if phase == 1:
                return "y", lambda i, h: W.at[g, x, i, pl.ds(2 * h, 2)], lambda n: W.at[g, x, 0:n]
            return "x", lambda i, h: W.at[g, i, pl.ds(2 * h, 2)], lambda n: W.at[g, 0:n]
        if phase == 1:
            return "x", lambda i, h: W.at[g, i, y, pl.ds(2 * h, 2)], lambda n: W.at[g, 0:n, y]
        return "y", lambda i, h: W.at[g, pl.ds(2 * h, 2), i], lambda n: W.at[g, :, 0:n]

    def rec(g, phase):
        return rec_b.at[g] if phase == 1 else rec_c.at[g]

    def ring_start(g, phase):
        axis, slab, _ = layout(g, phase)
        i = coords[axis]
        right, left = (i + 1) % 4, (i + 3) % 4
        s, r = send.at[g, phase], rec(g, phase)
        remote(slab(i, 0), slab(i, 0), s, r.at[0], axis, right)
        remote(slab(i, 1), slab(i, 1), s, r.at[1], axis, left)
        remote(slab(i, 1), slab(i, 1), s, r.at[2], axis, right)
        remote(slab(i, 0), slab(i, 0), s, r.at[2], axis, left)

    def ring_pass(g, phase):
        axis, slab, _ = layout(g, phase)
        i = coords[axis]
        right, left = (i + 1) % 4, (i + 3) % 4
        s, r = send.at[g, phase], rec(g, phase)
        wait(slab(left, 0), r.at[0])
        remote(slab(left, 0), slab(left, 0), s, r.at[2], axis, right)
        wait(slab(right, 1), r.at[1])
        remote(slab(right, 1), slab(right, 1), s, r.at[2], axis, left)

    def ring_wait(g, phase):
        wait(layout(g, phase)[2](2), rec(g, phase).at[2])

    b_start, b_pass, b_wait = (functools.partial(f, phase=1) for f in (ring_start, ring_pass, ring_wait))
    c_start, c_pass, c_wait = (functools.partial(f, phase=2) for f in (ring_start, ring_pass, ring_wait))

    def line_send(g, step, up):
        slab = W.at[g, :, :, z - step if up else z + step]
        k = step * 2 + (0 if up else 1)
        return pltpu.make_async_remote_copy(
            src_ref=slab, dst_ref=slab, send_sem=line_s.at[g - 8, k], recv_sem=line_r.at[g - 8, k],
            device_id=peer("z", z + 1 if up else z - 1), device_id_type=MESH,
        )

    def sends_up(step):
        return (z >= step) & (z < 3)

    def sends_down(step):
        return (z <= 3 - step) & (z > 0)

    def line_step(g, step):
        if step > 0:
            line_take(g, step - 1)
        if step < 3:
            @pl.when(sends_up(step))
            def _():
                line_send(g, step, True).start()

            @pl.when(sends_down(step))
            def _():
                line_send(g, step, False).start()

    def line_take(g, step):
        @pl.when(z >= step + 1)
        def _():
            wait(W.at[g, :, :, z - step - 1], line_r.at[g - 8, step * 2])

        @pl.when(z <= 2 - step)
        def _():
            wait(W.at[g, :, :, z + step + 1], line_r.at[g - 8, step * 2 + 1])

    def project(g0, g1):
        acc[...] = jnp.zeros_like(acc)

        def step(i, carry):
            w = jnp.concatenate(
                [W[g0, i].reshape(2048, HD), W[g1, i].reshape(2048, HD)], axis=1
            )
            acc[...] += jnp.dot(hid[i], w, preferred_element_type=jnp.float32)
            return carry

        lax.fori_loop(0, 4, step, 0)

    def rotated(v):
        return v * cosine[...] + pltpu.roll(v, HD // 2, 1) * sine[...]

    def queries(g0, g1):
        project(g0, g1)
        qs[g0 - 2] = rotated(acc[:, :HD]).astype(jnp.bfloat16)
        qs[g1 - 2] = rotated(acc[:, HD:]).astype(jnp.bfloat16)

    factor = math.log2(math.e) / math.sqrt(HD)
    last = (((1,), (1,)), ((), ()))

    def attend(g0):
        far_bias = flag[0] * neg_large

        def one(k, carry):
            h = g0 - 2 + k
            far_key = r4[0:2].reshape(TOK, HD)
            far_value = r4[2:4].reshape(TOK, HD)
            for b in range(2):
                n = 256 * (b + 1)
                q = qs[h, b * 256:n, :]
                own = lax.dot_general(q, ks[0:n, :], last, preferred_element_type=jnp.float32)
                rows = lax.broadcasted_iota(jnp.int32, (256, n), 0) + b * 256
                columns = lax.broadcasted_iota(jnp.int32, (256, n), 1)
                own = jnp.where(rows >= columns, own, neg_large)
                far = lax.dot_general(q, far_key, last, preferred_element_type=jnp.float32)
                far = far + far_bias
                top = jnp.maximum(
                    jnp.max(own, -1, keepdims=True), jnp.max(far, -1, keepdims=True)
                )
                own = jnp.exp2((own - top) * factor)
                far = jnp.exp2((far - top) * factor)
                total = jnp.sum(own, -1, keepdims=True) + jnp.sum(far, -1, keepdims=True)
                scale = 1.0 / total
                result = jnp.dot(
                    (own * scale).astype(jnp.bfloat16), vs[0:n, :],
                    preferred_element_type=jnp.float32,
                )
                result += jnp.dot(
                    (far * scale).astype(jnp.bfloat16), far_value,
                    preferred_element_type=jnp.float32,
                )
                att[h, b * 256:n, :] = result.astype(jnp.bfloat16)
            return carry

        lax.fori_loop(0, 2, one, 0)
        for h in (g0 - 2, g0 - 1):
            out_copy(h).start()

    def out_copy(h):
        return pltpu.make_async_copy(att.at[h], attended.at[:, pl.ds(h * HD, HD)], out_s.at[h])

    def page_own(step):
        if step == 0:
            return pltpu.make_async_copy(p1.at[x], p2.at[x], page_l.at[0])
        if step == 1:
            return pltpu.make_async_copy(p2.at[:, y], p3.at[pl.ds(y * 4, 4)], page_l.at[1])
        return pltpu.make_async_copy(p3.at[:, z], p4.at[pl.ds(z * 16, 16)], page_l.at[2])

    def page_start(step):
        axis = "xyz"[step]
        page_own(step).start()
        for d in (1, 3, 2):
            i = (coords[axis] + d) % 4
            if step == 0:
                src, dst = p1.at[i], p2.at[x]
            elif step == 1:
                src, dst = p2.at[:, i], p3.at[pl.ds(y * 4, 4)]
            else:
                src, dst = p3.at[:, i], p4.at[pl.ds(z * 16, 16)]
            remote(src, dst, page_s.at[step], page_r.at[step], axis, i)

    def page_wait(step, sem):
        wait((p2.at[0:3], p3.at[0:12], p4.at[0:48])[step], sem.at[step])

    def page_take(step):
        page_own(step).wait()
        page_wait(step, page_r)

    anchor_steps = (
        ("x", m0, r0), ("y", m1, r1), ("z", None, r2), ("y", None, r3), ("x", None, r4),
    )

    def anchor_start(step):
        axis, parts, to = anchor_steps[step]
        i = coords[axis]
        if step == 0:
            r0[x] = m0[x]
        elif step == 1:
            total = r0[0] + r0[1] + r0[2] + r0[3]
            m1[...] = total.reshape(4, 64, HD)
            r1[y] = m1[y]
        elif step == 2:
            m2[...] = r1[0] + r1[1] + r1[2] + r1[3]
            r2[z] = m2[...]
        elif step == 3:
            r3[y] = r2[0] + r2[1] + r2[2] + r2[3]
        else:
            r4[x] = r3[...].reshape(256, HD)
        for d in (1, 3, 2):
            j = (i + d) % 4
            src = parts.at[j] if parts is not None else to.at[i]
            remote(src, to.at[i], anc_s.at[step], anc_r.at[step], axis, j)

    def anchor_wait(step, sem):
        wait(anchor_steps[step][2].at[0:3], sem.at[step])

    def anchor_take(step):
        anchor_wait(step, anc_r)

    def keys_values():
        project(0, 1)
        key = rotated(acc[:, :HD]).astype(jnp.bfloat16)
        value = acc[:, HD:].astype(jnp.bfloat16)
        ks[...] = key
        vs[...] = value
        root = flag[0]
        wide_key, wide_value = key.astype(jnp.float32), value.astype(jnp.float32)
        m0[0:2] = (wide_key * root).astype(jnp.bfloat16).reshape(2, 256, HD)
        m0[2:4] = (wide_value * root).astype(jnp.bfloat16).reshape(2, 256, HD)
        pg[0:64, :, 0:HD] = wide_key.reshape(64, PAGE, HD)
        pg[0:64, :, HD:2 * HD] = wide_value.reshape(64, PAGE, HD)
        pg[64] = jnp.zeros((PAGE, 2 * HD), jnp.float32)

    def deal_pages():
        def one(o, carry):
            pair = jnp.concatenate([pg[page_src[2 * o]], pg[page_src[2 * o + 1]]], axis=0)
            p1[o // 16, (o // 4) % 4, o % 4] = pair.astype(jnp.bfloat16)
            return carry

        lax.fori_loop(0, 64, one, 0)

    def place_pages():
        def one(b, carry):
            kvo[b] = p4[source_of[b]]
            return carry

        lax.fori_loop(0, 64, one, 0)

    kv_copy = pltpu.make_async_copy(kvo, kv_cache, out_s.at[8])

    def each(f, *groups):
        for g in groups:
            f(g)

    each(a_start, 0, 1, 8, 9, 2, 3)
    for copy in hid_copies:
        copy.start()
    for g in (0, 1, 8, 9):
        a_wait(g)
        b_start(g)
    each(b_pass, 0, 1)
    for g in (0, 1):
        b_wait(g)
        c_start(g)
    b_pass(8)
    b_wait(8)
    line_step(8, 0)
    for g in (2, 3):
        a_wait(g)
        b_start(g)
    b_pass(9)
    b_wait(9)
    each(a_start, 4, 5)
    each(c_pass, 0, 1)
    each(b_pass, 2, 3)
    line_step(8, 1)
    line_step(9, 0)
    for g in (2, 3):
        b_wait(g)
        c_start(g)
    each(c_wait, 0, 1)
    for copy in hid_copies:
        copy.wait()
    keys_values()
    anchor_start(0)
    deal_pages()
    page_start(0)
    for g in (4, 5):
        a_wait(g)
        b_start(g)
    each(a_start, 6, 7)
    anchor_take(0)
    anchor_start(1)
    each(c_pass, 2, 3)
    line_step(8, 2)
    page_take(0)
    page_start(1)
    anchor_take(1)
    anchor_start(2)
    each(b_pass, 4, 5)
    for g in (4, 5):
        b_wait(g)
        c_start(g)
    page_take(1)
    page_start(2)
    anchor_take(2)
    anchor_start(3)
    each(c_wait, 2, 3)
    queries(2, 3)
    anchor_take(3)
    anchor_start(4)
    line_step(9, 1)
    for g in (6, 7):
        a_wait(g)
        b_start(g)
    each(c_pass, 4, 5)
    line_step(8, 3)
    anchor_take(4)
    each(b_pass, 6, 7)
    for g in (6, 7):
        b_wait(g)
        c_start(g)
    attend(2)
    line_step(9, 2)
    each(c_wait, 4, 5)
    queries(4, 5)
    each(c_pass, 6, 7)
    attend(4)
    page_take(2)
    place_pages()
    kv_copy.start()
    line_step(9, 3)
    queries(8, 9)
    attend(8)
    each(c_wait, 6, 7)
    queries(6, 7)
    attend(6)

    for g in range(10):
        wait(W.at[g, 0, 0, 0:3], send.at[g, 0])
        wait(layout(g, 1)[2](3), send.at[g, 1])
        if g < 8:
            wait(layout(g, 2)[2](3), send.at[g, 2])
    for g in (8, 9):
        for step in range(3):
            @pl.when(sends_up(step))
            def _():
                line_send(g, step, True).wait_send()

            @pl.when(sends_down(step))
            def _():
                line_send(g, step, False).wait_send()
    for step in range(3):
        page_wait(step, page_s)
    for step in range(5):
        anchor_wait(step, anc_s)
    for h in range(8):
        out_copy(h).wait()
    kv_copy.wait()


def on_device(hidden, w_query, w_key, w_value, block_order, page_map):
    ctx_count = lax.axis_size("ctx")
    my_block = block_order[lax.axis_index("ctx")]
    half = HD // 2
    exponent = jnp.arange(half, dtype=jnp.float32) * (2.0 / HD)
    inverse = jnp.exp(-exponent * jnp.log(jnp.float32(rope_theta)))
    positions = (my_block * TOK + jnp.arange(TOK, dtype=jnp.int32)).astype(jnp.float32)
    angles = positions[:, None] * inverse[None, :]
    cosine, sine = jnp.cos(angles), jnp.sin(angles)
    cosine = jnp.concatenate([cosine, cosine], -1)
    sine = jnp.concatenate([-sine, sine], -1)

    pages = TOK // PAGE
    owners = lax.dynamic_slice_in_dim(page_map[:, 0], my_block * pages, pages, 0)
    number = jnp.arange(pages, dtype=jnp.int32)
    same = owners[:, None] == owners[None, :]
    rank = jnp.sum((same & (number[None, :] < number[:, None])).astype(jnp.int32), -1)
    slot = owners * 2 + rank
    match = slot[None, :] == jnp.arange(2 * ctx_count, dtype=jnp.int32)[:, None]
    page_src = pages + jnp.sum(jnp.where(match, number[None, :] - pages, 0), -1)
    where = jnp.arange(ctx_count, dtype=jnp.int32)
    arrived = (where % 4) * 16 + ((where // 4) % 4) * 4 + where // 16
    source_of = jnp.sum(
        jnp.where(block_order[None, :] == where[:, None], arrived[None, :], 0), -1
    )
    flag = (my_block == 0).astype(jnp.float32).reshape(1)

    hbm = pl.BlockSpec(memory_space=pl.ANY)
    vmem = pl.BlockSpec(memory_space=pltpu.VMEM)
    smem = pl.BlockSpec(memory_space=pltpu.SMEM)
    bf16, f32, dma = jnp.bfloat16, jnp.float32, pltpu.SemaphoreType.DMA
    attended, kv = pl.pallas_call(
        kernel,
        out_shape=(
            jax.ShapeDtypeStruct((TOK, 8 * HD), bf16),
            jax.ShapeDtypeStruct((64, 16, 2 * HD), bf16),
        ),
        in_specs=[hbm] * 4 + [vmem] * 2 + [smem] * 3,
        out_specs=(hbm, hbm),
        scratch_shapes=[
            pltpu.VMEM((10, 4, 4, 4, 128, 128), bf16),
            pltpu.VMEM((4, TOK, 2048), bf16),
            pltpu.VMEM((TOK, 256), f32),
            pltpu.VMEM((TOK, HD), bf16),
            pltpu.VMEM((TOK, HD), bf16),
            pltpu.VMEM((8, TOK, HD), bf16),
            pltpu.VMEM((8, TOK, HD), bf16),
            pltpu.VMEM((65, PAGE, 2 * HD), f32),
            pltpu.VMEM((4, 4, 4, 16, 2 * HD), bf16),
            pltpu.VMEM((4, 4, 4, 16, 2 * HD), bf16),
            pltpu.VMEM((16, 4, 16, 2 * HD), bf16),
            pltpu.VMEM((64, 16, 2 * HD), bf16),
            pltpu.VMEM((4, 256, HD), bf16),
            pltpu.VMEM((4, 256, HD), bf16),
            pltpu.VMEM((4, 64, HD), bf16),
            pltpu.VMEM((4, 64, HD), bf16),
            pltpu.VMEM((64, HD), bf16),
            pltpu.VMEM((4, 64, HD), bf16),
            pltpu.VMEM((4, 64, HD), bf16),
            pltpu.VMEM((4, 256, HD), bf16),
            pltpu.VMEM((64, 16, 2 * HD), bf16),
            dma((14,)),
            dma((10, 3)),
            dma((10,)),
            dma((10, 3)),
            dma((8, 3)),
            dma((2, 6)),
            dma((2, 6)),
            dma((3,)),
            dma((3,)),
            dma((3,)),
            dma((5,)),
            dma((5,)),
            dma((9,)),
        ],
        compiler_params=pltpu.CompilerParams(
            collective_id=0, has_side_effects=True, vmem_limit_bytes=56 * 1024 * 1024
        ),
        cost_estimate=pl.CostEstimate(
            flops=2 * TOK * 8192 * 1280, bytes_accessed=12 << 20, transcendentals=8 * TOK * 1024
        ),
    )(hidden, w_query, w_key, w_value, cosine, sine, page_src, source_of, flag)
    return attended, kv.reshape(1, ctx_count, 2, PAGE, 2 * HD)


def solution(mesh):
    placed = (P("ctx", None), P("ctx", "tp"), P("ctx", "tp"), P("ctx", "tp"), P(), P())
    return jax.shard_map(
        on_device,
        mesh=mesh,
        in_specs=placed,
        out_specs=(P("ctx", "tp"), P("ctx", None, None, None, "tp")),
        check_vma=False,
    )
```

time: 1800 us -> 155 us (0.09)
  the two profiles are of different devices: /device:TPU:32 before, /device:TPU:8 now
where the time goes in v1:
time: 155 us
  Pallas kernels  141 us (91%)
  local copies, waits for them, and re-layouts  6.1 us (4%)
  other arithmetic  4.93 us (3%)
  between operations  2.6 us (2%)
    pallas_call x1, Pallas kernels, on_device(): pl.pallas_call(kernel, out_shape=(jax.ShapeDtypeStruct((TOK, 8 * HD), bf1...  141 us
    unnamed x2, local copies, waits for them, and re-layouts  4.13 us

profile of v1, /device:TPU:8, one launch (start us, length us, event | category | flops | bytes accessed | tf_op | source)
XLA Modules:
  0.0 154.7 jit_solution(768537076422098949)
XLA Ops:
  0.6 1.2 dynamic_slice.8
  3.8 0.7 dynamic-slice_bitcast_fusion
  4.6 0.2 convert_reduce_fusion
  4.7 0.7 iota_add_fusion
  5.5 0.1 select_reduce_fusion.1
  5.6 0.5 broadcast_add_fusion.page_src
  6.1 1.4 select_reduce_fusion.source_of
  7.5 1.0 fusion
  8.5 1.0 pad_maximum_fusion
  9.5 141.1 %shard_map.77 = (bf16[512,1024]{1,0:T(8,128)(2,1)}, bf16[64,16,256]{2,1,0:T(8,128)(2,1)}) custom-call(bf16[512,8192]{1,0:T(8,128)(2,1)} %hidden.1, bf16[128,1024]{1,0:T(8,128)(2,1)} %w_query.1, bf16[128,128]{1,0:T(8,128)(2,1)} %w_key.1, bf16[128,128]{1,0:T(8,128)(2,1)} %w_value.1, f32[512,128]{1,0:T(8,128)} %get-tuple-element.9.cosine, ...), custom_call_target="tpu_custom_call" | custom-call | flops 10737418240 | bytes 12582912 | tf_op jit(solution)/shard_map/pallas_call | solution.py:455
  150.6 2.3 %copy.10 = bf16[512,1024]{1,0:T(8,128)(2,1)} copy(bf16[512,1024]{1,0:T(8,128)(2,1)} %get-tuple-element.15) | data formatting | bytes 2097152
  152.8 1.9 %copy.11 = bf16[1,64,2,8,256]{4,3,2,1,0:T(8,128)(2,1)} copy(bf16[1,64,2,8,256]{4,3,2,1,0:T(8,128)(2,1)} %bitcast.7) | data formatting | bytes 1048576
  (3 shorter events, 0.0 us)

commit v2 on v1

--- a/solution.py
+++ b/solution.py
@@ -20,13 +20,19 @@
 def kernel(
     hidden, w_query, w_key, w_value, cosine, sine, page_src, source_of, flag,
     attended, kv_cache,
-    W, hid, acc, ks, vs, qs, att, pg, p1, p2, p3, p4, m0, r0, m1, r1, m2, r2, r3, r4, kvo,
-    loc, send, rec_a, rec_b, rec_c, line_s, line_r, page_s, page_r, page_l, anc_s, anc_r, out_s,
+    wkv, wq, hid, hid_p, acc, q_own, part_s, part_r,
+    kt, vs, qs, att, pg, p1, p2, p3, p4, m0, r0, m1, r1, r2, r3, r4, kvo,
+    loc, hid_l, send, rec_a, rec_b, rec_c, hid_s, hid_r, core_s, core_r, par_s, par_r,
+    page_s, page_r, page_l, anc_s, anc_r, out_s,
 ):
     c = lax.axis_index("ctx")
     x = c // 16
     y = (c // 4) % 4
     z = c % 4
+    half, parity = z // 2, z % 2
+    beside = z + 1 - 2 * parity
+    tp = lax.axis_index("tp")
+    core = tp % 2
     coords = {"x": x, "y": y, "z": z}
 
     def peer(axis, i):
@@ -44,6 +50,9 @@
 
     def wait(ref, sem):
         pltpu.make_async_copy(ref, ref, sem).wait()
+
+    def mine(g):
+        return wkv.at[g, x, y, z] if g < 2 else wq.at[g - 2, x, y, half]
 
     def own_copy(g):
         if g == 0:
@@ -52,14 +61,20 @@
             src = w_value
         else:
             src = w_query.at[:, pl.ds((g - 2) * HD, HD)]
-        return pltpu.make_async_copy(src, W.at[g, x, y, z], loc.at[g])
-
-    hid_copies = [
-        pltpu.make_async_copy(hidden.at[:, pl.ds(i * 2048, 2048)], hid.at[i], loc.at[10 + i])
-        for i in range(4)
-    ]
-    for g in (0, 1, 8, 9, 2, 3, 4, 5, 6, 7):
+        return pltpu.make_async_copy(src, mine(g), loc.at[g])
+
+    for g in range(10):
         own_copy(g).start()
+
+    def hid_load(k, carry):
+        pltpu.make_async_copy(
+            hidden.at[:, pl.ds(pl.multiple_of(k * HD, HD), HD)],
+            hid.at[k // 16, (k // 4) % 4, (k // 2) % 2, k % 2],
+            hid_l.at[0],
+        ).start()
+        return carry
+
+    lax.fori_loop(0, 64, hid_load, 0)
 
     barrier = pltpu.get_barrier_semaphore()
     for axis in "xyz":
@@ -67,31 +82,42 @@
             pl.semaphore_signal(
                 barrier, inc=1, device_id=peer(axis, (coords[axis] + d) % 4), device_id_type=MESH
             )
-    pl.semaphore_wait(barrier, 9)
-
-    def first_axis(g):
-        return "x" if g >= 8 else "z"
+    pl.semaphore_signal(
+        barrier, inc=1, device_id={"tp": tp + 1 - 2 * core}, device_id_type=MESH
+    )
+    pl.semaphore_wait(barrier, 10)
 
     def a_start(g):
         own_copy(g).wait()
-        axis = first_axis(g)
-        mine = W.at[g, x, y, z]
-        for d in (1, 3, 2):
-            remote(mine, mine, send.at[g, 0], rec_a.at[g], axis, (coords[axis] + d) % 4)
+        if g < 2:
+            for d in (1, 3, 2):
+                remote(mine(g), mine(g), send.at[g, 0], rec_a.at[g], "z", (z + d) % 4)
+        else:
+            remote(mine(g), mine(g), send.at[g, 0], rec_a.at[g], "z", (z + 2) % 4)
+
+    def a_done(g, sem):
+        wait(wkv.at[g, x, y, 0:3] if g < 2 else wq.at[g - 2, x, y, 0], sem)
 
     def a_wait(g):
-        wait(W.at[g, x, y, 0:3], rec_a.at[g])
+        a_done(g, rec_a.at[g])
 
     def layout(g, phase):
-        if g >= 8:
-            return "y", lambda i, h: W.at[g, pl.ds(2 * h, 2), i, z], lambda n: W.at[g, :, 0:n, z]
+        w, k, n_half = (wkv, g, 2) if g < 2 else (wq, g - 2, 1)
         if g % 2 == 0:
             if phase == 1:
-                return "y", lambda i, h: W.at[g, x, i, pl.ds(2 * h, 2)], lambda n: W.at[g, x, 0:n]
-            return "x", lambda i, h: W.at[g, i, pl.ds(2 * h, 2)], lambda n: W.at[g, 0:n]
+                return (
+                    "y",
+                    lambda i, h: w.at[k, x, i, pl.ds(n_half * h, n_half)],
+                    lambda n: w.at[k, x, 0:n],
+                )
+            return "x", lambda i, h: w.at[k, i, pl.ds(2 * h, 2)], lambda n: w.at[k, 0:n]
         if phase == 1:
-            return "x", lambda i, h: W.at[g, i, y, pl.ds(2 * h, 2)], lambda n: W.at[g, 0:n, y]
-        return "y", lambda i, h: W.at[g, pl.ds(2 * h, 2), i], lambda n: W.at[g, :, 0:n]
+            return (
+                "x",
+                lambda i, h: w.at[k, i, y, pl.ds(n_half * h, n_half)],
+                lambda n: w.at[k, 0:n, y],
+            )
+        return "y", lambda i, h: w.at[k, pl.ds(2 * h, 2), i], lambda n: w.at[k, :, 0:n]
 
     def rec(g, phase):
         return rec_b.at[g] if phase == 1 else rec_c.at[g]
@@ -122,99 +148,109 @@
     b_start, b_pass, b_wait = (functools.partial(f, phase=1) for f in (ring_start, ring_pass, ring_wait))
     c_start, c_pass, c_wait = (functools.partial(f, phase=2) for f in (ring_start, ring_pass, ring_wait))
 
-    def line_send(g, step, up):
-        slab = W.at[g, :, :, z - step if up else z + step]
-        k = step * 2 + (0 if up else 1)
-        return pltpu.make_async_remote_copy(
-            src_ref=slab, dst_ref=slab, send_sem=line_s.at[g - 8, k], recv_sem=line_r.at[g - 8, k],
-            device_id=peer("z", z + 1 if up else z - 1), device_id_type=MESH,
+    def hid_piece(ref, k):
+        return ref.at[k // 2, pl.ds(2 * (k % 2), 2)]
+
+    def hid_start(j):
+        k = core * 4 + j
+        remote(
+            hid.at[k // 2, pl.ds(2 * (k % 2), 2), :, 1 - parity], hid_piece(hid_p, k),
+            hid_s.at[0], hid_r.at[j], "z", beside,
         )
 
-    def sends_up(step):
-        return (z >= step) & (z < 3)
-
-    def sends_down(step):
-        return (z <= 3 - step) & (z > 0)
-
-    def line_step(g, step):
-        if step > 0:
-            line_take(g, step - 1)
-        if step < 3:
-            @pl.when(sends_up(step))
-            def _():
-                line_send(g, step, True).start()
-
-            @pl.when(sends_down(step))
-            def _():
-                line_send(g, step, False).start()
-
-    def line_take(g, step):
-        @pl.when(z >= step + 1)
-        def _():
-            wait(W.at[g, :, :, z - step - 1], line_r.at[g - 8, step * 2])
-
-        @pl.when(z <= 2 - step)
-        def _():
-            wait(W.at[g, :, :, z + step + 1], line_r.at[g - 8, step * 2 + 1])
-
-    def project(g0, g1):
-        acc[...] = jnp.zeros_like(acc)
-
-        def step(i, carry):
-            w = jnp.concatenate(
-                [W[g0, i].reshape(2048, HD), W[g1, i].reshape(2048, HD)], axis=1
+    def hid_pass(j):
+        k = core * 4 + j
+        piece = hid_piece(hid_p, k)
+        wait(piece, hid_r.at[j])
+        pltpu.make_async_remote_copy(
+            src_ref=piece, dst_ref=piece, send_sem=core_s.at[0], recv_sem=core_r.at[0],
+            device_id={"tp": tp + 1 - 2 * core}, device_id_type=MESH,
+        ).start()
+
+    def project(left_of, k, w, pieces):
+        rows = pieces * HD
+        total = None
+        for i in range(4):
+            right = jnp.concatenate(
+                [w[k, i].reshape(rows, HD), w[k + 1, i].reshape(rows, HD)], axis=1
             )
-            acc[...] += jnp.dot(hid[i], w, preferred_element_type=jnp.float32)
-            return carry
-
-        lax.fori_loop(0, 4, step, 0)
+            d = jnp.dot(left_of(i), right, preferred_element_type=jnp.float32)
+            total = d if total is None else total + d
+        acc[...] = total
+
+    def all_hidden(i):
+        return jnp.concatenate(
+            [hid[i, b, e, f] for b in range(4) for e in range(2) for f in range(2)], axis=1
+        )
+
+    def own_hidden(i):
+        return jnp.concatenate(
+            [hid[i, b, e, parity] for b in range(4) for e in range(2)], axis=1
+        )
+
+    def other_hidden(i):
+        return jnp.concatenate([hid_p[i, b, e] for b in range(4) for e in range(2)], axis=1)
 
     def rotated(v):
         return v * cosine[...] + pltpu.roll(v, HD // 2, 1) * sine[...]
 
-    def queries(g0, g1):
-        project(g0, g1)
-        qs[g0 - 2] = rotated(acc[:, :HD]).astype(jnp.bfloat16)
-        qs[g1 - 2] = rotated(acc[:, HD:]).astype(jnp.bfloat16)
+    def parts_other(g):
+        h = g - 2
+        project(other_hidden, h, wq, 8)
+        part_s[h] = acc[:, :HD].astype(jnp.bfloat16)
+        part_s[h + 1] = acc[:, HD:].astype(jnp.bfloat16)
+        pair = pl.ds(h, 2)
+        remote(part_s.at[pair], part_r.at[pair], par_s.at[h // 2], par_r.at[h // 2], "z", beside)
+
+    def parts_own(g):
+        h = g - 2
+        project(own_hidden, h, wq, 8)
+        q_own[h] = acc[:, :HD]
+        q_own[h + 1] = acc[:, HD:]
+
+    def part_wait(h, sem):
+        wait(part_r.at[pl.ds(h, 2)], sem.at[h // 2])
+
+    def queries(g):
+        part_wait(g - 2, par_r)
+        for h in (g - 2, g - 1):
+            qs[h] = rotated(q_own[h] + part_r[h].astype(jnp.float32)).astype(jnp.bfloat16)
 
     factor = math.log2(math.e) / math.sqrt(HD)
-    last = (((1,), (1,)), ((), ()))
+
+    def anchor_ready():
+        kt[:, 0:TOK] = r4[0:2].reshape(TOK, HD).astype(jnp.float32).T.astype(jnp.bfloat16)
+        vs[0:TOK, 0:HD] = r4[2:4].reshape(TOK, HD)
+        vs[:, HD:] = jnp.ones((2 * TOK, HD), jnp.bfloat16)
 
     def attend(g0):
         far_bias = flag[0] * neg_large
 
         def one(k, carry):
             h = g0 - 2 + k
-            far_key = r4[0:2].reshape(TOK, HD)
-            far_value = r4[2:4].reshape(TOK, HD)
             for b in range(2):
-                n = 256 * (b + 1)
-                q = qs[h, b * 256:n, :]
-                own = lax.dot_general(q, ks[0:n, :], last, preferred_element_type=jnp.float32)
-                rows = lax.broadcasted_iota(jnp.int32, (256, n), 0) + b * 256
-                columns = lax.broadcasted_iota(jnp.int32, (256, n), 1)
-                own = jnp.where(rows >= columns, own, neg_large)
-                far = lax.dot_general(q, far_key, last, preferred_element_type=jnp.float32)
-                far = far + far_bias
-                top = jnp.maximum(
-                    jnp.max(own, -1, keepdims=True), jnp.max(far, -1, keepdims=True)
+                n = 768 + 256 * b
+                q = qs[h, b * 256:b * 256 + 256, :]
+                scores = jnp.dot(q, kt[:, 0:n], preferred_element_type=jnp.float32)
+                rows = lax.broadcasted_iota(jnp.int32, (256, 256), 0)
+                columns = lax.broadcasted_iota(jnp.int32, (256, 256), 1)
+                last = jnp.where(rows >= columns, scores[:, n - 256:], neg_large)
+                far = scores[:, 0:TOK] + far_bias
+                pieces = [far, last] if b == 0 else [far, scores[:, TOK:n - 256], last]
+                top = functools.reduce(
+                    jnp.maximum, [jnp.max(v, -1, keepdims=True) for v in pieces]
                 )
-                own = jnp.exp2((own - top) * factor)
-                far = jnp.exp2((far - top) * factor)
-                total = jnp.sum(own, -1, keepdims=True) + jnp.sum(far, -1, keepdims=True)
-                scale = 1.0 / total
-                result = jnp.dot(
-                    (own * scale).astype(jnp.bfloat16), vs[0:n, :],
-                    preferred_element_type=jnp.float32,
+                weights = jnp.concatenate(
+                    [jnp.exp2((v - top) * factor).astype(jnp.bfloat16) for v in pieces], axis=1
                 )
-                result += jnp.dot(
-                    (far * scale).astype(jnp.bfloat16), far_value,
-                    preferred_element_type=jnp.float32,
-                )
-                att[h, b * 256:n, :] = result.astype(jnp.bfloat16)
+                result = jnp.dot(weights, vs[0:n, :], preferred_element_type=jnp.float32)
+                att[h, b * 256:b * 256 + 256, :] = (
+                    result[:, 0:HD] / result[:, HD:]
+                ).astype(jnp.bfloat16)
             return carry
 
-        lax.fori_loop(0, 2, one, 0)
+        one(0, 0)
+        one(1, 0)
         for h in (g0 - 2, g0 - 1):
             out_copy(h).start()
 
@@ -262,8 +298,7 @@
             m1[...] = total.reshape(4, 64, HD)
             r1[y] = m1[y]
         elif step == 2:
-            m2[...] = r1[0] + r1[1] + r1[2] + r1[3]
-            r2[z] = m2[...]
+            r2[z] = r1[0] + r1[1] + r1[2] + r1[3]
         elif step == 3:
             r3[y] = r2[0] + r2[1] + r2[2] + r2[3]
         else:
@@ -280,13 +315,13 @@
         anchor_wait(step, anc_r)
 
     def keys_values():
-        project(0, 1)
+        project(all_hidden, 0, wkv, 16)
         key = rotated(acc[:, :HD]).astype(jnp.bfloat16)
         value = acc[:, HD:].astype(jnp.bfloat16)
-        ks[...] = key
-        vs[...] = value
         root = flag[0]
         wide_key, wide_value = key.astype(jnp.float32), value.astype(jnp.float32)
+        kt[:, TOK:] = wide_key.T.astype(jnp.bfloat16)
+        vs[TOK:, 0:HD] = value
         m0[0:2] = (wide_key * root).astype(jnp.bfloat16).reshape(2, 256, HD)
         m0[2:4] = (wide_value * root).astype(jnp.bfloat16).reshape(2, 256, HD)
         pg[0:64, :, 0:HD] = wide_key.reshape(64, PAGE, HD)
@@ -314,104 +349,106 @@
         for g in groups:
             f(g)
 
-    each(a_start, 0, 1, 8, 9, 2, 3)
-    for copy in hid_copies:
-        copy.start()
-    for g in (0, 1, 8, 9):
+    each(a_start, 0, 1)
+    for g in (0, 1):
         a_wait(g)
         b_start(g)
+    each(a_start, *range(2, 10))
+    wait(hid, hid_l.at[0])
+    each(hid_start, 0, 1, 2, 3)
     each(b_pass, 0, 1)
     for g in (0, 1):
         b_wait(g)
         c_start(g)
-    b_pass(8)
-    b_wait(8)
-    line_step(8, 0)
     for g in (2, 3):
         a_wait(g)
         b_start(g)
-    b_pass(9)
-    b_wait(9)
-    each(a_start, 4, 5)
     each(c_pass, 0, 1)
+    for g in (4, 5):
+        a_wait(g)
+        b_start(g)
     each(b_pass, 2, 3)
-    line_step(8, 1)
-    line_step(9, 0)
     for g in (2, 3):
         b_wait(g)
         c_start(g)
+    each(b_pass, 4, 5)
+    hid_pass(0)
     each(c_wait, 0, 1)
-    for copy in hid_copies:
-        copy.wait()
     keys_values()
     anchor_start(0)
+    each(c_pass, 2, 3)
+    for g in (6, 7):
+        a_wait(g)
+        b_start(g)
     deal_pages()
     page_start(0)
     for g in (4, 5):
+        b_wait(g)
+        c_start(g)
+    hid_pass(1)
+    each(b_pass, 6, 7)
+    anchor_take(0)
+    anchor_start(1)
+    each(c_wait, 2, 3)
+    parts_own(2)
+    each(c_pass, 4, 5)
+    for g in (8, 9):
         a_wait(g)
         b_start(g)
-    each(a_start, 6, 7)
-    anchor_take(0)
-    anchor_start(1)
-    each(c_pass, 2, 3)
-    line_step(8, 2)
+    hid_pass(2)
     page_take(0)
     page_start(1)
     anchor_take(1)
     anchor_start(2)
-    each(b_pass, 4, 5)
-    for g in (4, 5):
-        b_wait(g)
-        c_start(g)
-    page_take(1)
-    page_start(2)
-    anchor_take(2)
-    anchor_start(3)
-    each(c_wait, 2, 3)
-    queries(2, 3)
-    anchor_take(3)
-    anchor_start(4)
-    line_step(9, 1)
-    for g in (6, 7):
-        a_wait(g)
-        b_start(g)
-    each(c_pass, 4, 5)
-    line_step(8, 3)
-    anchor_take(4)
-    each(b_pass, 6, 7)
     for g in (6, 7):
         b_wait(g)
         c_start(g)
+    each(b_pass, 8, 9)
+    anchor_take(2)
+    anchor_start(3)
+    hid_pass(3)
+    each(c_wait, 4, 5)
+    each(c_pass, 6, 7)
+    parts_own(4)
+    for g in (8, 9):
+        b_wait(g)
+        c_start(g)
+    anchor_take(3)
+    anchor_start(4)
+    wait(hid_p.at[0:2], core_r.at[0])
+    parts_other(2)
+    parts_other(4)
+    page_take(1)
+    page_start(2)
+    each(c_wait, 6, 7)
+    parts_other(6)
+    each(c_pass, 8, 9)
+    parts_own(6)
+    anchor_take(4)
+    anchor_ready()
+    queries(2)
     attend(2)
-    line_step(9, 2)
-    each(c_wait, 4, 5)
-    queries(4, 5)
-    each(c_pass, 6, 7)
+    queries(4)
     attend(4)
+    each(c_wait, 8, 9)
+    parts_other(8)
+    parts_own(8)
+    queries(6)
+    attend(6)
     page_take(2)
     place_pages()
     kv_copy.start()
-    line_step(9, 3)
-    queries(8, 9)
+    queries(8)
     attend(8)
-    each(c_wait, 6, 7)
-    queries(6, 7)
-    attend(6)
 
     for g in range(10):
-        wait(W.at[g, 0, 0, 0:3], send.at[g, 0])
+        a_done(g, send.at[g, 0])
         wait(layout(g, 1)[2](3), send.at[g, 1])
-        if g < 8:
-            wait(layout(g, 2)[2](3), send.at[g, 2])
-    for g in (8, 9):
-        for step in range(3):
-            @pl.when(sends_up(step))
-            def _():
-                line_send(g, step, True).wait_send()
-
-            @pl.when(sends_down(step))
-            def _():
-                line_send(g, step, False).wait_send()
+        wait(layout(g, 2)[2](3), send.at[g, 2])
+    wait(hid_p.at[0:2], hid_s.at[0])
+    wait(hid_p.at[0:2], core_s.at[0])
+    for h in (0, 2, 4, 6):
+        part_wait(h, par_s)
     for step in range(3):
         page_wait(step, page_s)
     for step in range(5):
@@ -461,11 +498,16 @@
         in_specs=[hbm] * 4 + [vmem] * 2 + [smem] * 3,
         out_specs=(hbm, hbm),
         scratch_shapes=[
-            pltpu.VMEM((10, 4, 4, 4, 128, 128), bf16),
-            pltpu.VMEM((4, TOK, 2048), bf16),
-            pltpu.VMEM((TOK, 256), f32),
-            pltpu.VMEM((TOK, HD), bf16),
-            pltpu.VMEM((TOK, HD), bf16),
+            pltpu.VMEM((2, 4, 4, 4, HD, HD), bf16),
+            pltpu.VMEM((8, 4, 4, 2, HD, HD), bf16),
+            pltpu.VMEM((4, 4, 2, 2, TOK, HD), bf16),
+            pltpu.VMEM((4, 4, 2, TOK, HD), bf16),
+            pltpu.VMEM((TOK, 2 * HD), f32),
+            pltpu.VMEM((8, TOK, HD), f32),
+            pltpu.VMEM((8, TOK, HD), bf16),
+            pltpu.VMEM((8, TOK, HD), bf16),
+            pltpu.VMEM((HD, 2 * TOK), bf16),
+            pltpu.VMEM((2 * TOK, 2 * HD), bf16),
             pltpu.VMEM((8, TOK, HD), bf16),
             pltpu.VMEM((8, TOK, HD), bf16),
             pltpu.VMEM((65, PAGE, 2 * HD), f32),
@@ -477,18 +519,22 @@
             pltpu.VMEM((4, 256, HD), bf16),
             pltpu.VMEM((4, 64, HD), bf16),
             pltpu.VMEM((4, 64, HD), bf16),
-            pltpu.VMEM((64, HD), bf16),
             pltpu.VMEM((4, 64, HD), bf16),
             pltpu.VMEM((4, 64, HD), bf16),
             pltpu.VMEM((4, 256, HD), bf16),
             pltpu.VMEM((64, 16, 2 * HD), bf16),
-            dma((14,)),
+            dma((10,)),
+            dma((1,)),
             dma((10, 3)),
             dma((10,)),
             dma((10, 3)),
-            dma((8, 3)),
-            dma((2, 6)),
-            dma((2, 6)),
+            dma((10, 3)),
+            dma((1,)),
+            dma((4,)),
+            dma((1,)),
+            dma((1,)),
+            dma((4,)),
+            dma((4,)),
             dma((3,)),
             dma((3,)),
             dma((3,)),

time: 155 us -> 133 us (0.86)
  the two profiles are of different devices: /device:TPU:8 before, /device:TPU:32 now
where the time goes in v2:
time: 133 us
  Pallas kernels  119 us (89%)
  local copies, waits for them, and re-layouts  6.1 us (5%)
  other arithmetic  4.93 us (4%)
  between operations  2.6 us (2%)
    pallas_call x1, Pallas kernels, on_device(): pl.pallas_call(kernel, out_shape=(jax.ShapeDtypeStruct((TOK, 8 * HD), bf1...  119 us
    unnamed x2, local copies, waits for them, and re-layouts  4.13 us

profile of v2, /device:TPU:32, one launch (start us, length us, event | category | flops | bytes accessed | tf_op | source)
XLA Modules:
  0.0 133.1 jit_solution(4133046207356601457)
XLA Ops:
  0.6 1.2 dynamic_slice.8
  3.8 0.7 dynamic-slice_bitcast_fusion
  4.6 0.2 convert_reduce_fusion
  4.7 0.7 iota_add_fusion
  5.5 0.1 select_reduce_fusion.1
  5.6 0.5 broadcast_add_fusion.page_src
  6.1 1.4 %select_reduce_fusion.source_of = s32[64]{0:T(128)} fusion(s32[64]{0:T(128)S(1)} %fusion.4, s32[64]{0:T(128)} %param.10), kind=kLoop, calls=%fused_computation.5 | loop fusion | flops 12224 | bytes 768 | tf_op jit(solution)/shard_map/reduce_sum | solution.py:483
  7.5 1.0 fusion
  8.5 1.0 pad_maximum_fusion
  9.5 119.5 %shard_map.77 = (bf16[512,1024]{1,0:T(8,128)(2,1)}, bf16[64,16,256]{2,1,0:T(8,128)(2,1)}) custom-call(bf16[512,8192]{1,0:T(8,128)(2,1)} %hidden.1, bf16[128,1024]{1,0:T(8,128)(2,1)} %w_query.1, bf16[128,128]{1,0:T(8,128)(2,1)} %w_key.1, bf16[128,128]{1,0:T(8,128)(2,1)} %w_value.1, f32[512,128]{1,0:T(8,128)} %get-tuple-element.9.cosine, ...), custom_call_target="tpu_custom_call" | custom-call | flops 10737418240 | bytes 12582912 | tf_op jit(solution)/shard_map/pallas_call | solution.py:492
  129.0 2.3 %copy.10 = bf16[512,1024]{1,0:T(8,128)(2,1)} copy(bf16[512,1024]{1,0:T(8,128)(2,1)} %get-tuple-element.15) | data formatting | bytes 2097152
  131.3 1.9 %copy.11 = bf16[1,64,2,8,256]{4,3,2,1,0:T(8,128)(2,1)} copy(bf16[1,64,2,8,256]{4,3,2,1,0:T(8,128)(2,1)} %bitcast.7) | data formatting | bytes 1048576
  (3 shorter events, 0.0 us)

commit v3 on v2

--- a/solution.py
+++ b/solution.py
@@ -3,6 +3,7 @@
 
 import jax
 import jax.numpy as jnp
+import numpy as np
 from jax import lax
 from jax.experimental import pallas as pl
 from jax.experimental.pallas import tpu as pltpu
@@ -18,10 +19,11 @@
 
 
 def kernel(
-    hidden, w_query, w_key, w_value, cosine, sine, page_src, source_of, flag,
+    hidden, w_query, w_key, w_value, inverse, block_order, page_map,
     attended, kv_cache,
     wkv, wq, hid, hid_p, acc, q_own, part_s, part_r,
-    kt, vs, qs, att, pg, p1, p2, p3, p4, m0, r0, m1, r1, r2, r3, r4, kvo,
+    cosine, sine, kt, vs, qs, att, pg, p1, p2, p3, p4, m0, r0, m1, r1, r2, r3, r4, kvo,
+    to_owner, to_block,
     loc, hid_l, send, rec_a, rec_b, rec_c, hid_s, hid_r, core_s, core_r, par_s, par_r,
     page_s, page_r, page_l, anc_s, anc_r, out_s,
 ):
@@ -34,6 +36,8 @@
     tp = lax.axis_index("tp")
     core = tp % 2
     coords = {"x": x, "y": y, "z": z}
+    my_block = block_order[c]
+    root = jnp.where(my_block == 0, 1.0, 0.0).astype(jnp.float32)
 
     def peer(axis, i):
         if axis == "x":
@@ -224,7 +228,7 @@
         vs[:, HD:] = jnp.ones((2 * TOK, HD), jnp.bfloat16)
 
     def attend(g0):
-        far_bias = flag[0] * neg_large
+        far_bias = root * neg_large
 
         def one(k, carry):
             h = g0 - 2 + k
@@ -318,30 +322,63 @@
         project(all_hidden, 0, wkv, 16)
         key = rotated(acc[:, :HD]).astype(jnp.bfloat16)
         value = acc[:, HD:].astype(jnp.bfloat16)
-        root = flag[0]
         wide_key, wide_value = key.astype(jnp.float32), value.astype(jnp.float32)
         kt[:, TOK:] = wide_key.T.astype(jnp.bfloat16)
         vs[TOK:, 0:HD] = value
         m0[0:2] = (wide_key * root).astype(jnp.bfloat16).reshape(2, 256, HD)
         m0[2:4] = (wide_value * root).astype(jnp.bfloat16).reshape(2, 256, HD)
-        pg[0:64, :, 0:HD] = wide_key.reshape(64, PAGE, HD)
-        pg[0:64, :, HD:2 * HD] = wide_value.reshape(64, PAGE, HD)
-        pg[64] = jnp.zeros((PAGE, 2 * HD), jnp.float32)
+        pg[:, 0:HD] = key
+        pg[:, HD:] = value
+
+    def angles():
+        row = lax.broadcasted_iota(jnp.int32, (TOK, HD), 0)
+        angle = (my_block * TOK + row).astype(jnp.float32) * inverse[...]
+        lane = lax.broadcasted_iota(jnp.int32, (TOK, HD), 1)
+        cosine[...] = jnp.cos(angle)
+        turned = jnp.sin(angle)
+        sine[...] = jnp.where(lane < HD // 2, -turned, turned)
+
+    def spread_lanes(count, width, value_of):
+        lane = lax.broadcasted_iota(jnp.int32, (1, count * width), 1)
+
+        def one(k, row):
+            return jnp.where(lane // width == k, value_of(k), row)
+
+        return lane, lax.fori_loop(0, count, one, jnp.zeros_like(lane))
+
+    def one_hot(rows, target):
+        row = lax.broadcasted_iota(jnp.int32, (rows, target.shape[1]), 0)
+        return jnp.where(row == target, 1.0, 0.0).astype(jnp.bfloat16)
+
+    def page_targets():
+        def owner(j):
+            return page_map[my_block * 64 + j]
+
+        lane, owners = spread_lanes(64, PAGE, owner)
+
+        def rank(j, total):
+            later = (owners == owner(j)) & (lane // PAGE > j)
+            return total + jnp.where(later, 1, 0)
+
+        ranks = lax.fori_loop(0, 64, rank, jnp.zeros_like(owners))
+        to_owner[...] = (owners * 2 + ranks) * PAGE + lane % PAGE
+        lane, blocks = spread_lanes(
+            64, 16, lambda a: block_order[(a % 4) * 16 + (a // 4) % 4 * 4 + a // 16]
+        )
+        to_block[...] = blocks * 16 + lane % 16
 
     def deal_pages():
-        def one(o, carry):
-            pair = jnp.concatenate([pg[page_src[2 * o]], pg[page_src[2 * o + 1]]], axis=0)
-            p1[o // 16, (o // 4) % 4, o % 4] = pair.astype(jnp.bfloat16)
-            return carry
-
-        lax.fori_loop(0, 64, one, 0)
+        dealt = jnp.dot(
+            one_hot(1024, to_owner[...]), pg[...], preferred_element_type=jnp.float32
+        )
+        p1[...] = dealt.astype(jnp.bfloat16).reshape(4, 4, 4, 16, 2 * HD)
 
     def place_pages():
-        def one(b, carry):
-            kvo[b] = p4[source_of[b]]
-            return carry
-
-        lax.fori_loop(0, 64, one, 0)
+        placed = jnp.dot(
+            one_hot(1024, to_block[...]), p4[...].reshape(1024, 2 * HD),
+            preferred_element_type=jnp.float32,
+        )
+        kvo[...] = placed.astype(jnp.bfloat16).reshape(64, 16, 2 * HD)
 
     kv_copy = pltpu.make_async_copy(kvo, kv_cache, out_s.at[8])
 
@@ -363,6 +400,8 @@
     for g in (2, 3):
         a_wait(g)
         b_start(g)
+    page_targets()
+    angles()
     each(c_pass, 0, 1)
     for g in (4, 5):
         a_wait(g)
@@ -460,30 +499,8 @@
 
 def on_device(hidden, w_query, w_key, w_value, block_order, page_map):
     ctx_count = lax.axis_size("ctx")
-    my_block = block_order[lax.axis_index("ctx")]
-    half = HD // 2
-    exponent = jnp.arange(half, dtype=jnp.float32) * (2.0 / HD)
-    inverse = jnp.exp(-exponent * jnp.log(jnp.float32(rope_theta)))
-    positions = (my_block * TOK + jnp.arange(TOK, dtype=jnp.int32)).astype(jnp.float32)
-    angles = positions[:, None] * inverse[None, :]
-    cosine, sine = jnp.cos(angles), jnp.sin(angles)
-    cosine = jnp.concatenate([cosine, cosine], -1)
-    sine = jnp.concatenate([-sine, sine], -1)
-
-    pages = TOK // PAGE
-    owners = lax.dynamic_slice_in_dim(page_map[:, 0], my_block * pages, pages, 0)
-    number = jnp.arange(pages, dtype=jnp.int32)
-    same = owners[:, None] == owners[None, :]
-    rank = jnp.sum((same & (number[None, :] < number[:, None])).astype(jnp.int32), -1)
-    slot = owners * 2 + rank
-    match = slot[None, :] == jnp.arange(2 * ctx_count, dtype=jnp.int32)[:, None]
-    page_src = pages + jnp.sum(jnp.where(match, number[None, :] - pages, 0), -1)
-    where = jnp.arange(ctx_count, dtype=jnp.int32)
-    arrived = (where % 4) * 16 + ((where // 4) % 4) * 4 + where // 16
-    source_of = jnp.sum(
-        jnp.where(block_order[None, :] == where[:, None], arrived[None, :], 0), -1
-    )
-    flag = (my_block == 0).astype(jnp.float32).reshape(1)
+    exponent = np.arange(HD, dtype=np.float64) % (HD // 2) * (2.0 / HD)
+    inverse = jnp.asarray((rope_theta ** -exponent).astype(np.float32)[None, :])
 
     hbm = pl.BlockSpec(memory_space=pl.ANY)
     vmem = pl.BlockSpec(memory_space=pltpu.VMEM)
@@ -495,7 +512,7 @@
             jax.ShapeDtypeStruct((TOK, 8 * HD), bf16),
             jax.ShapeDtypeStruct((64, 16, 2 * HD), bf16),
         ),
-        in_specs=[hbm] * 4 + [vmem] * 2 + [smem] * 3,
+        in_specs=[hbm] * 4 + [vmem] + [smem] * 2,
         out_specs=(hbm, hbm),
         scratch_shapes=[
             pltpu.VMEM((2, 4, 4, 4, HD, HD), bf16),
@@ -506,11 +523,13 @@
             pltpu.VMEM((8, TOK, HD), f32),
             pltpu.VMEM((8, TOK, HD), bf16),
             pltpu.VMEM((8, TOK, HD), bf16),
+            pltpu.VMEM((TOK, HD), f32),
+            pltpu.VMEM((TOK, HD), f32),
             pltpu.VMEM((HD, 2 * TOK), bf16),
             pltpu.VMEM((2 * TOK, 2 * HD), bf16),
             pltpu.VMEM((8, TOK, HD), bf16),
             pltpu.VMEM((8, TOK, HD), bf16),
-            pltpu.VMEM((65, PAGE, 2 * HD), f32),
+            pltpu.VMEM((TOK, 2 * HD), bf16),
             pltpu.VMEM((4, 4, 4, 16, 2 * HD), bf16),
             pltpu.VMEM((4, 4, 4, 16, 2 * HD), bf16),
             pltpu.VMEM((16, 4, 16, 2 * HD), bf16),
@@ -523,6 +542,8 @@
             pltpu.VMEM((4, 64, HD), bf16),
             pltpu.VMEM((4, 256, HD), bf16),
             pltpu.VMEM((64, 16, 2 * HD), bf16),
+            pltpu.VMEM((1, TOK), jnp.int32),
+            pltpu.VMEM((1, 1024), jnp.int32),
             dma((10,)),
             dma((1,)),
             dma((10, 3)),
@@ -548,7 +569,7 @@
         cost_estimate=pl.CostEstimate(
             flops=2 * TOK * 8192 * 1280, bytes_accessed=12 << 20, transcendentals=8 * TOK * 1024
         ),
-    )(hidden, w_query, w_key, w_value, cosine, sine, page_src, source_of, flag)
+    )(hidden, w_query, w_key, w_value, inverse, block_order, page_map[:, 0])
     return attended, kv.reshape(1, ctx_count, 2, PAGE, 2 * HD)
 
 

time: 133 us -> 126 us (0.947)
  other arithmetic: 4.93 us -> 0 us
  Pallas kernels: 119 us -> 121 us
  local copies, waits for them, and re-layouts: 6.1 us -> 4.13 us
  between operations: 2.6 us -> 0.64 us
    dynamic_slice x2 -> x0, local copies, waits for them, and re-layouts: 1.97 us -> none  [the longest x1 1.24 us: on_device(): my_block = block_order[lax.axis_index('ctx')]]
    reduce_sum x3 -> x0, other arithmetic: 1.63 us -> none  [the longest x1 1.36 us: on_device(): jnp.sum(jnp.where(block_order[None, :] == where[:, None], arrived[None, :...]
where the time goes in v3:
time: 126 us; the launch traced here: 125 us
  Pallas kernels  121 us (96%)
  local copies, waits for them, and re-layouts  4.13 us (3%)
    pallas_call x1, Pallas kernels, on_device(): pl.pallas_call(kernel, out_shape=(jax.ShapeDtypeStruct((TOK, 8 * HD), bf1...  121 us
    unnamed x2, local copies, waits for them, and re-layouts  4.13 us

profile of v3, /device:TPU:32, one launch (start us, length us, event | category | flops | bytes accessed | tf_op | source)
XLA Modules:
  0.0 125.3 jit_solution(4586736230348114671)
XLA Ops:
  0.6 120.5 %shard_map.86 = (bf16[512,1024]{1,0:T(8,128)(2,1)}, bf16[64,16,256]{2,1,0:T(8,128)(2,1)}) custom-call(bf16[512,8192]{1,0:T(8,128)(2,1)} %hidden.1, bf16[128,1024]{1,0:T(8,128)(2,1)} %w_query.1, bf16[128,128]{1,0:T(8,128)(2,1)} %w_key.1, bf16[128,128]{1,0:T(8,128)(2,1)} %w_value.1, f32[1,128]{1,0:T(1,128)} %constant.2.clone.inverse, s32[64]{0:T(128)} %block_order.1, ...), custom_call_target="tpu_custom_call" | custom-call | flops 10737418240 | bytes 12582912 | tf_op jit(solution)/shard_map/pallas_call | solution.py:509
  121.1 2.3 %copy.11 = bf16[512,1024]{1,0:T(8,128)(2,1)} copy(bf16[512,1024]{1,0:T(8,128)(2,1)} %get-tuple-element.8) | data formatting | bytes 2097152
  123.4 1.9 %copy.12 = bf16[1,64,2,8,256]{4,3,2,1,0:T(8,128)(2,1)} copy(bf16[1,64,2,8,256]{4,3,2,1,0:T(8,128)(2,1)} %bitcast.2) | data formatting | bytes 1048576

commit v4 on v3

--- a/solution.py
+++ b/solution.py
@@ -421,44 +421,42 @@
         b_start(g)
     deal_pages()
     page_start(0)
-    for g in (4, 5):
-        b_wait(g)
-        c_start(g)
+    each(b_wait, 4, 5)
     hid_pass(1)
+    each(c_start, 4, 5)
     each(b_pass, 6, 7)
     anchor_take(0)
     anchor_start(1)
     each(c_wait, 2, 3)
+    hid_pass(2)
     parts_own(2)
     each(c_pass, 4, 5)
     for g in (8, 9):
         a_wait(g)
         b_start(g)
-    hid_pass(2)
     page_take(0)
     page_start(1)
     anchor_take(1)
     anchor_start(2)
-    for g in (6, 7):
-        b_wait(g)
-        c_start(g)
+    each(b_wait, 6, 7)
+    hid_pass(3)
+    each(c_start, 6, 7)
     each(b_pass, 8, 9)
     anchor_take(2)
     anchor_start(3)
-    hid_pass(3)
+    page_take(1)
+    page_start(2)
     each(c_wait, 4, 5)
     each(c_pass, 6, 7)
-    parts_own(4)
+    wait(hid_p.at[0:2], core_r.at[0])
+    parts_other(2)
+    parts_other(4)
     for g in (8, 9):
         b_wait(g)
         c_start(g)
     anchor_take(3)
     anchor_start(4)
-    wait(hid_p.at[0:2], core_r.at[0])
-    parts_other(2)
-    parts_other(4)
-    page_take(1)
-    page_start(2)
+    parts_own(4)
     each(c_wait, 6, 7)
     parts_other(6)
     each(c_pass, 8, 9)

time: 126 us -> 118 us (0.937)
  Pallas kernels: 121 us -> 112 us
    pallas_call x1, Pallas kernels: 121 us -> 112 us  [on_device(): pl.pallas_call(kernel, out_shape=(jax.ShapeDtypeStruct((TOK, 8 * HD), bf1...]
where the time goes in v4:
time: 118 us; the launch traced here: 117 us
  Pallas kernels  112 us (95%)
  local copies, waits for them, and re-layouts  4.13 us (4%)
    pallas_call x1, Pallas kernels, on_device(): pl.pallas_call(kernel, out_shape=(jax.ShapeDtypeStruct((TOK, 8 * HD), bf1...  112 us
    unnamed x2, local copies, waits for them, and re-layouts  4.13 us

profile of v4, /device:TPU:32, one launch (start us, length us, event | category | flops | bytes accessed | tf_op | source)
XLA Modules:
  0.0 117.0 jit_solution(170644353292581338)
XLA Ops:
  0.6 112.2 %shard_map.86 = (bf16[512,1024]{1,0:T(8,128)(2,1)}, bf16[64,16,256]{2,1,0:T(8,128)(2,1)}) custom-call(bf16[512,8192]{1,0:T(8,128)(2,1)} %hidden.1, bf16[128,1024]{1,0:T(8,128)(2,1)} %w_query.1, bf16[128,128]{1,0:T(8,128)(2,1)} %w_key.1, bf16[128,128]{1,0:T(8,128)(2,1)} %w_value.1, f32[1,128]{1,0:T(1,128)} %constant.2.clone.inverse, s32[64]{0:T(128)} %block_order.1, ...), custom_call_target="tpu_custom_call" | custom-call | flops 10737418240 | bytes 12582912 | tf_op jit(solution)/shard_map/pallas_call | solution.py:507
  112.8 2.3 %copy.11 = bf16[512,1024]{1,0:T(8,128)(2,1)} copy(bf16[512,1024]{1,0:T(8,128)(2,1)} %get-tuple-element.8) | data formatting | bytes 2097152
  115.1 1.9 %copy.12 = bf16[1,64,2,8,256]{4,3,2,1,0:T(8,128)(2,1)} copy(bf16[1,64,2,8,256]{4,3,2,1,0:T(8,128)(2,1)} %bitcast.2) | data formatting | bytes 1048576

commit v5 on v4

--- a/solution.py
+++ b/solution.py
@@ -67,7 +67,7 @@
             src = w_query.at[:, pl.ds((g - 2) * HD, HD)]
         return pltpu.make_async_copy(src, mine(g), loc.at[g])
 
-    for g in range(10):
+    for g in range(2):
         own_copy(g).start()
 
     def hid_load(k, carry):
@@ -77,8 +77,6 @@
             hid_l.at[0],
         ).start()
         return carry
-
-    lax.fori_loop(0, 64, hid_load, 0)
 
     barrier = pltpu.get_barrier_semaphore()
     for axis in "xyz":
@@ -203,8 +201,8 @@
         project(other_hidden, h, wq, 8)
         part_s[h] = acc[:, :HD].astype(jnp.bfloat16)
         part_s[h + 1] = acc[:, HD:].astype(jnp.bfloat16)
-        pair = pl.ds(h, 2)
-        remote(part_s.at[pair], part_r.at[pair], par_s.at[h // 2], par_r.at[h // 2], "z", beside)
+        for k in (h, h + 1):
+            remote(part_s.at[k], part_r.at[k], par_s.at[k], par_r.at[k], "z", beside)
 
     def parts_own(g):
         h = g - 2
@@ -213,12 +211,15 @@
         q_own[h + 1] = acc[:, HD:]
 
     def part_wait(h, sem):
-        wait(part_r.at[pl.ds(h, 2)], sem.at[h // 2])
+        wait(part_r.at[h], sem.at[h])
+
+    def query(h):
+        part_wait(h, par_r)
+        qs[h] = rotated(q_own[h] + part_r[h].astype(jnp.float32)).astype(jnp.bfloat16)
 
     def queries(g):
-        part_wait(g - 2, par_r)
-        for h in (g - 2, g - 1):
-            qs[h] = rotated(q_own[h] + part_r[h].astype(jnp.float32)).astype(jnp.bfloat16)
+        query(g - 2)
+        query(g - 1)
 
     factor = math.log2(math.e) / math.sqrt(HD)
 
@@ -227,11 +228,10 @@
         vs[0:TOK, 0:HD] = r4[2:4].reshape(TOK, HD)
         vs[:, HD:] = jnp.ones((2 * TOK, HD), jnp.bfloat16)
 
-    def attend(g0):
+    def attend(*heads):
         far_bias = root * neg_large
 
-        def one(k, carry):
-            h = g0 - 2 + k
+        def one(h):
             for b in range(2):
                 n = 768 + 256 * b
                 q = qs[h, b * 256:b * 256 + 256, :]
@@ -251,11 +251,10 @@
                 att[h, b * 256:b * 256 + 256, :] = (
                     result[:, 0:HD] / result[:, HD:]
                 ).astype(jnp.bfloat16)
-            return carry
-
-        one(0, 0)
-        one(1, 0)
-        for h in (g0 - 2, g0 - 1):
+
+        for h in heads:
+            one(h)
+        for h in heads:
             out_copy(h).start()
 
     def out_copy(h):
@@ -387,6 +386,9 @@
             f(g)
 
     each(a_start, 0, 1)
+    for g in range(2, 10):
+        own_copy(g).start()
+    lax.fori_loop(0, 64, hid_load, 0)
     for g in (0, 1):
         a_wait(g)
         b_start(g)
@@ -464,19 +466,20 @@
     anchor_take(4)
     anchor_ready()
     queries(2)
-    attend(2)
+    attend(0, 1)
     queries(4)
-    attend(4)
+    attend(2, 3)
     each(c_wait, 8, 9)
     parts_other(8)
     parts_own(8)
     queries(6)
-    attend(6)
+    attend(4, 5)
     page_take(2)
     place_pages()
     kv_copy.start()
-    queries(8)
-    attend(8)
+    for h in (6, 7):
+        query(h)
+        attend(h)
 
     for g in range(10):
         a_done(g, send.at[g, 0])
@@ -484,7 +487,7 @@
         wait(layout(g, 2)[2](3), send.at[g, 2])
     wait(hid_p.at[0:2], hid_s.at[0])
     wait(hid_p.at[0:2], core_s.at[0])
-    for h in (0, 2, 4, 6):
+    for h in range(8):
         part_wait(h, par_s)
     for step in range(3):
         page_wait(step, page_s)
@@ -552,8 +555,8 @@
             dma((4,)),
             dma((1,)),
             dma((1,)),
-            dma((4,)),
-            dma((4,)),
+            dma((8,)),
+            dma((8,)),
             dma((3,)),
             dma((3,)),
             dma((3,)),

time: 118 us -> 116 us (0.983)
    pallas_call x1, Pallas kernels: 112 us -> 111 us  [on_device(): pl.pallas_call(kernel, out_shape=(jax.ShapeDtypeStruct((TOK, 8 * HD), bf1...]
where the time goes in v5:
time: 116 us
  Pallas kernels  111 us (96%)
  local copies, waits for them, and re-layouts  4.13 us (4%)
    pallas_call x1, Pallas kernels, on_device(): pl.pallas_call(kernel, out_shape=(jax.ShapeDtypeStruct((TOK, 8 * HD), bf1...  111 us
    unnamed x2, local copies, waits for them, and re-layouts  4.13 us

profile of v5, /device:TPU:32, one launch (start us, length us, event | category | flops | bytes accessed | tf_op | source)
XLA Modules:
  0.0 115.6 jit_solution(3507396621326089362)
XLA Ops:
  0.6 110.8 %shard_map.86 = (bf16[512,1024]{1,0:T(8,128)(2,1)}, bf16[64,16,256]{2,1,0:T(8,128)(2,1)}) custom-call(bf16[512,8192]{1,0:T(8,128)(2,1)} %hidden.1, bf16[128,1024]{1,0:T(8,128)(2,1)} %w_query.1, bf16[128,128]{1,0:T(8,128)(2,1)} %w_key.1, bf16[128,128]{1,0:T(8,128)(2,1)} %w_value.1, f32[1,128]{1,0:T(1,128)} %constant.2.clone.inverse, s32[64]{0:T(128)} %block_order.1, ...), custom_call_target="tpu_custom_call" | custom-call | flops 10737418240 | bytes 12582912 | tf_op jit(solution)/shard_map/pallas_call | solution.py:510
  111.4 2.3 %copy.11 = bf16[512,1024]{1,0:T(8,128)(2,1)} copy(bf16[512,1024]{1,0:T(8,128)(2,1)} %get-tuple-element.8) | data formatting | bytes 2097152
  113.7 1.9 %copy.12 = bf16[1,64,2,8,256]{4,3,2,1,0:T(8,128)(2,1)} copy(bf16[1,64,2,8,256]{4,3,2,1,0:T(8,128)(2,1)} %bitcast.2) | data formatting | bytes 1048576
